TPU v7x, 32 devices: a whole 2x2x4 slice. The times are simulated.
32 devices in a mesh: sub: 8 (over z, y), fac: 4 (over x, core).
Axes of the slice: x: 2, y: 2, z: 4, core: 2. Of those that a mesh axis runs over, the one named last changes fastest.
Arguments:
- visibility: bfloat16 [12288, 256], P(('sub', 'fac')), may hold values from -6 to 6
- vis_weight: bfloat16 [12288, 128], P(('sub', 'fac')), may hold values from 0.099609375 to 1
- tap_start: int32 [12288, 2], P(('sub', 'fac')), may hold values from 4096 to 127999
- tap_step: int32 [12288, 2], P(('sub', 'fac')), may hold values from 102 to 818
- subgrid_id: int32 [12288], P(('sub', 'fac')), may hold values from 0 to 23, as said below
- w_plane: int32 [12288], P(('sub', 'fac')), may hold values from 0 to 3
- tile_intersection: int32 [24, 2], P('sub'), may hold values from 0 to 7936, as said below
Outputs:
- uv_planes: float32 [4, 2, 1024, 8192], P('fac', None, 'sub')
Inputs may be any that keep to these rules, and one draw needn't show every extreme that they name: Within the rows of one device at most 8 rows name the same pair of subgrid_id and w_plane, and one pair is named by exactly 8 rows of every device. `tile_intersection`: column 0 is below 128; column 1 is at most 7936.
All inputs are finite; a program needn't handle non-finite values.
Results may differ from a plain program's by a relative error of at most 0.0038.
Values may be sent and summed in bfloat16 or wider, within the bound.
A program may use at most 64 MiB of HBM per device.

v0:
```python
import functools
import math

import jax
import jax.numpy as jnp
from jax import lax
from jax.experimental import pallas as pl
from jax.experimental.pallas import tpu as pltpu
from jax.sharding import PartitionSpec as P

SG = 256
GS = 8192
BAND = 128
LANES = 128
BATCH = 8
VMEM_LIMIT = 48 * 1024 * 1024
PACK_LIMIT = 63 * 1024 * 1024

kernel_norm = 1.6e-07
SERIES = [kernel_norm * 81.0**k / math.factorial(k) ** 2 for k in range(1, 40)]

NT = (((1,), (1,)), ((), ()))
NN = (((1,), (0,)), ((), ()))


def iota(shape, axis):
    return lax.broadcasted_iota(jnp.int32, shape, axis)


def onehot(mask):
    return jnp.where(mask, 1.0, 0.0).astype(jnp.bfloat16)


def dot(a, b, dims=NN):
    return lax.dot_general(a, b, dims, preferred_element_type=jnp.float32)


def pack_kernel(capacity, dest_count, members, planes, subgrid, plane, vis, weight, start, step, packet):
    rows = vis.shape[0]
    slots = packet.shape[0]
    subgrids, w_planes = subgrid[...].reshape(1, rows), plane[...].reshape(1, rows)
    sub = jnp.floor((subgrids.astype(jnp.float32) + 0.5) * (1.0 / members)).astype(jnp.int32)
    goal = (sub * planes + w_planes) * members + subgrids - sub * members
    named = iota((dest_count, rows), 0) == goal
    ahead = onehot(iota((rows, rows), 0) < iota((rows, rows), 1))
    before = dot(onehot(named), ahead)
    rank = jnp.sum(jnp.where(named, before, 0.0), axis=0, keepdims=True)
    slot = goal * capacity + rank.astype(jnp.int32)
    place = onehot(iota((slots, rows), 0) == slot)
    line = iota((LANES, rows), 0)
    begin, pace = start[...], step[...]
    value = jnp.where(line < 3, begin[0:1], begin[1:2])
    value = jnp.where(line < 6, value, pace[0:1])
    value = jnp.where(line < 8, value, pace[1:2])
    piece = jnp.where(line < 3, line, line - 3)
    piece = jnp.where(line < 6, piece, line - 6)
    piece = jnp.where(line < 8, piece, line - 8)
    piece = jnp.minimum(piece, 3) * 8
    value = jnp.right_shift(value, piece) & 255
    value = jnp.where(line < 10, value, jnp.where(line == 10, 1, 0))
    track = value.astype(jnp.float32).astype(jnp.bfloat16)
    packet[:, 0 : 2 * LANES] = dot(place, vis[...]).astype(jnp.bfloat16)
    packet[:, 2 * LANES : 3 * LANES] = dot(place, weight[...]).astype(jnp.bfloat16)
    packet[:, 3 * LANES : 4 * LANES] = dot(place, track, NT).astype(jnp.bfloat16)


def exchange_kernel(sub_count, fac_count, source, landed, send_sem, recv_sem, own_sem):
    count = sub_count * fac_count
    me = lax.axis_index("sub") * fac_count + lax.axis_index("fac")

    def peer(k):
        other = lax.rem(me + k, count)
        return other, (other // fac_count, lax.rem(other, fac_count))

    barrier = pltpu.get_barrier_semaphore()

    def greet(k, carry):
        pl.semaphore_signal(barrier, inc=1, device_id=peer(k)[1], device_id_type=pl.DeviceIdType.MESH)
        return carry

    lax.fori_loop(1, count, greet, 0)
    own = pltpu.make_async_copy(source.at[me], landed.at[me], own_sem)
    own.start()
    pl.semaphore_wait(barrier, count - 1)

    def transfer(k, block):
        other, where = peer(k)
        return pltpu.make_async_remote_copy(
            src_ref=source.at[other],
            dst_ref=landed.at[block],
            send_sem=send_sem.at[k],
            recv_sem=recv_sem.at[k],
            device_id=where,
            device_id_type=pl.DeviceIdType.MESH,
        )

    def send(k, carry):
        transfer(k, me).start()
        return carry

    def finish(k, carry):
        transfer(k, me).wait_send()
        transfer(k, lax.rem(me + count - k, count)).wait_recv()
        return carry

    lax.fori_loop(1, count, send, 0)
    lax.fori_loop(1, count, finish, 0)
    own.wait()


def sort_kernel(capacity, members, packet, scaled, position, counts):
    slots = packet.shape[0]
    part = slots // members
    track = packet[:, 3 * LANES : 4 * LANES]
    used = dot(onehot(iota((8, LANES), 1) == 10), track, NT)[0:1]
    slot = iota((1, slots), 1).astype(jnp.float32)
    group = jnp.floor((slot + 0.5) * (1.0 / capacity))
    cycle = jnp.floor((group + 0.5) * (1.0 / members))
    member = (group - cycle * members).astype(jnp.int32)
    ahead = onehot(iota((slots, slots), 0) < iota((slots, slots), 1))
    mine = (iota((8, slots), 0) == member) & (used > 0.5)
    before = dot(onehot(mine), ahead)
    rank = jnp.sum(jnp.where(mine, before, 0.0), axis=0, keepdims=True).astype(jnp.int32)
    goal = jnp.where(used > 0.5, member * part + rank, -1)
    place = onehot(iota((slots, slots), 0) == goal)
    for m in range(members):
        counts[m] = jnp.sum(jnp.where((member == m) & (used > 0.5), 1, 0))
    weight = dot(place, packet[:, 2 * LANES : 3 * LANES])
    scaled[:, 0:LANES] = dot(place, packet[:, 0:LANES]) * weight
    scaled[:, LANES : 2 * LANES] = dot(place, packet[:, LANES : 2 * LANES]) * weight
    line, chan = iota((LANES, LANES), 0), iota((LANES, LANES), 1)
    moved = dot(place, track).astype(jnp.bfloat16)
    for axis in range(2):
        mix = jnp.zeros((LANES, LANES), jnp.int32)
        for n in range(3):
            mix = jnp.where(line == 3 * axis + n, 256**n, mix)
        for n in range(2):
            mix = jnp.where(line == 6 + 2 * axis + n, chan * 256**n, mix)
        mix = mix.astype(jnp.float32).astype(jnp.bfloat16)
        position[:, axis * LANES : (axis + 1) * LANES] = dot(moved, mix).astype(jnp.int32)


def taps(place):
    shape = (place.shape[0], 8, LANES)
    spot = jnp.broadcast_to(place[:, None, :], shape)
    first = jnp.right_shift(spot, 10) - 3
    cell = first + ((iota(shape, 1) - first) & 7)
    offset = (cell * 1024 - spot).astype(jnp.float32) * (1.0 / 1024.0)
    inside = jnp.maximum(1.0 - offset * offset * 0.0625, 0.0)
    total = jnp.full(shape, SERIES[-1], jnp.float32)
    for term in SERIES[-2::-1]:
        total = total * inside + term
    return total * inside, cell


def halves(cell):
    block = jnp.right_shift(cell, 4)
    upper = (cell & 8) != 0
    low = jnp.where(upper, -1, block)
    high = jnp.where(upper, block, -1)
    return jnp.concatenate([low, high], axis=1).astype(jnp.int16)


def twice(value):
    return jnp.concatenate([value, value], axis=1).astype(jnp.bfloat16)


def grid_kernel(member, scaled, position, counts, corner, *refs):
    own, near, far, left_a, right_a, left_b, right_b, total = refs[-8:]
    last = scaled.shape[0] // BATCH - 1

    def build(b, left, right):
        rows = pl.ds(pl.multiple_of(jnp.minimum(b, last) * BATCH, BATCH), BATCH)
        tap_u, cell_u = taps(position[rows, 0:LANES])
        tap_v, cell_v = taps(position[rows, LANES : 2 * LANES])
        block_u, block_v = halves(cell_u), halves(cell_v)
        right_tap = twice(tap_u)
        real = twice(scaled[rows, 0:LANES][:, None, :] * tap_v)
        imag = twice(scaled[rows, LANES : 2 * LANES][:, None, :] * tap_v)
        zero = jnp.zeros((16, LANES), jnp.bfloat16)
        for r in range(BATCH):
            cols = slice(r * LANES, (r + 1) * LANES)
            for k in range(SG // 16):
                here = block_u[r] == jnp.int16(k)
                right[k * 16 : (k + 1) * 16, cols] = jnp.where(here, right_tap[r], zero)
                here = block_v[r] == jnp.int16(k)
                left[k * 16 : (k + 1) * 16, cols] = jnp.where(here, real[r], zero)
                left[SG + k * 16 : SG + (k + 1) * 16, cols] = jnp.where(here, imag[r], zero)

    def pair(i, carry):
        build(2 * i + 1, left_b, right_b)
        total[...] += dot(left_a[...], right_a[...], NT)
        build(2 * i + 2, left_a, right_a)
        total[...] += dot(left_b[...], right_b[...], NT)
        return carry

    total[...] = jnp.zeros_like(total)
    build(0, left_a, right_a)
    lax.fori_loop(0, (counts[member] + 2 * BATCH - 1) // (2 * BATCH), pair, 0)
    shift = corner[member, 0]
    for p in range(2):
        grid = total[p * SG : (p + 1) * SG, :]
        spread = jnp.concatenate([grid, jnp.zeros((BAND, SG), jnp.float32)], axis=0)
        spread = pltpu.roll(spread, shift, 0)
        own[p] = spread[0:BAND]
        near[p] = spread[BAND : 2 * BAND].astype(near.dtype)
        far[p] = spread[2 * BAND :].astype(far.dtype)


def place_kernel(count, columns, *refs):
    band = refs[-1]
    width = band.shape[-1]
    band[...] = jnp.zeros_like(band)
    for n, ref in enumerate(refs[:-1]):
        column = columns[n]
        base = jnp.minimum(lax.shift_right_logical(column, 7), (width - 3 * LANES) // LANES)
        piece = ref[0].astype(jnp.float32)
        piece = jnp.concatenate([piece, jnp.zeros((piece.shape[0], LANES), jnp.float32)], axis=1)
        piece = pltpu.roll(piece, column - base * LANES, 1)
        cols = pl.ds(pl.multiple_of(base * LANES, LANES), 3 * LANES)
        band[0, 0, :, cols] += piece


def params(limit=VMEM_LIMIT, **extra):
    return pltpu.CompilerParams(vmem_limit_bytes=limit, **extra)


def whole(count):
    return [pl.BlockSpec(memory_space=pltpu.VMEM)] * count


def shards(visibility, vis_weight, tap_start, tap_step, subgrid_id, w_plane, tile_intersection):
    sub_count = lax.axis_size("sub")
    fac_count = lax.axis_size("fac")
    rows, chans = vis_weight.shape
    members = tile_intersection.shape[0]
    dest_count = sub_count * fac_count * members
    capacity = max(2, (2 * rows + dest_count - 1) // dest_count)
    slots = dest_count * capacity
    part = slots // members
    smem = pl.BlockSpec(memory_space=pltpu.SMEM)

    columns = tile_intersection[:, 1]
    ring = lambda d: [((i - d) % sub_count, i) for i in range(sub_count)]
    next_cols = lax.ppermute(columns, "sub", ring(1))
    far_cols = lax.ppermute(columns, "sub", ring(2))

    packet = pl.pallas_call(
        functools.partial(pack_kernel, capacity, dest_count, members, fac_count),
        out_shape=jax.ShapeDtypeStruct((slots, 4 * LANES), jnp.bfloat16),
        grid=(1,),
        in_specs=[
            pl.BlockSpec((rows,), lambda i: (0,)),
            pl.BlockSpec((rows,), lambda i: (0,)),
            pl.BlockSpec((rows, 2 * chans), lambda i: (0, 0)),
            pl.BlockSpec((rows, chans), lambda i: (0, 0)),
            pl.BlockSpec((2, rows), lambda i: (0, 0)),
            pl.BlockSpec((2, rows), lambda i: (0, 0)),
        ],
        out_specs=pl.BlockSpec((slots, 4 * LANES), lambda i: (0, 0)),
        compiler_params=params(PACK_LIMIT),
    )(subgrid_id, w_plane, visibility, vis_weight, tap_start.T, tap_step.T)
    devices = sub_count * fac_count
    blocks = jax.ShapeDtypeStruct((devices, members * capacity, 4 * LANES), jnp.bfloat16)
    packet = pl.pallas_call(
        functools.partial(exchange_kernel, sub_count, fac_count),
        out_shape=blocks,
        in_specs=[pl.BlockSpec(memory_space=pl.ANY)],
        out_specs=whole(1)[0],
        scratch_shapes=[
            pltpu.SemaphoreType.DMA((devices,)),
            pltpu.SemaphoreType.DMA((devices,)),
            pltpu.SemaphoreType.DMA,
        ],
        compiler_params=params(collective_id=0, has_side_effects=True),
    )(packet.reshape(blocks.shape)).reshape(slots, 4 * LANES)
    scaled, position, counts = pl.pallas_call(
        functools.partial(sort_kernel, capacity, members),
        out_shape=(
            jax.ShapeDtypeStruct((slots, 2 * LANES), jnp.float32),
            jax.ShapeDtypeStruct((slots, 2 * LANES), jnp.int32),
            jax.ShapeDtypeStruct((members,), jnp.int32),
        ),
        in_specs=whole(1),
        out_specs=(*whole(2), smem),
        compiler_params=params(),
    )(packet)

    owns, nears, fars = [], [], []
    for m in range(members):
        arrived = (nears[m - 2], fars[m - 2]) if m >= 2 else (next_cols, far_cols) if m == 1 else ()
        block = pl.BlockSpec((part, 2 * LANES), lambda i, m=m: (m, 0))
        piece = pl.BlockSpec((2, BAND, SG), lambda i: (0, 0, 0))
        own, near, far = pl.pallas_call(
            functools.partial(grid_kernel, m),
            grid=(1,),
            out_shape=(
                jax.ShapeDtypeStruct((2, BAND, SG), jnp.float32),
                jax.ShapeDtypeStruct((2, BAND, SG), jnp.bfloat16),
                jax.ShapeDtypeStruct((2, BAND, SG), jnp.bfloat16),
            ),
            in_specs=[block, block, smem, smem] + [pl.BlockSpec(memory_space=pl.ANY)] * len(arrived),
            out_specs=(piece, piece, piece),
            scratch_shapes=[
                pltpu.VMEM((2 * SG, BATCH * LANES), jnp.bfloat16),
                pltpu.VMEM((SG, BATCH * LANES), jnp.bfloat16),
                pltpu.VMEM((2 * SG, BATCH * LANES), jnp.bfloat16),
                pltpu.VMEM((SG, BATCH * LANES), jnp.bfloat16),
                pltpu.VMEM((2 * SG, SG), jnp.float32),
            ],
            compiler_params=params(),
            cost_estimate=pl.CostEstimate(flops=1000, bytes_accessed=1000, transcendentals=0),
        )(scaled, position, counts, tile_intersection, *arrived)
        owns.append(own)
        nears.append(lax.ppermute(near, "sub", ring(1)))
        fars.append(lax.ppermute(far, "sub", ring(2)))

    places = jnp.concatenate([columns, next_cols, far_cols])
    high = 64
    cut = pl.BlockSpec((1, high, SG), lambda p, i: (p, i, 0))
    return pl.pallas_call(
        functools.partial(place_kernel, 3 * members),
        grid=(2, BAND // high),
        out_shape=jax.ShapeDtypeStruct((1, 2, BAND, GS), jnp.float32),
        in_specs=[smem] + [cut] * (3 * members),
        out_specs=pl.BlockSpec((1, 1, high, GS), lambda p, i: (0, p, i, 0)),
        compiler_params=params(),
    )(places, *owns, *nears, *fars)


def solution(mesh):
    placed = (
        P(("sub", "fac"), None),
        P(("sub", "fac"), None),
        P(("sub", "fac"), None),
        P(("sub", "fac"), None),
        P(("sub", "fac")),
        P(("sub", "fac")),
        P("sub", None),
    )
    return jax.shard_map(
        shards, mesh=mesh, in_specs=placed, out_specs=P("fac", None, "sub", None), check_vma=False
    )
```

profile of v0, /device:TPU:6, one launch (start us, length us, event | category | flops | bytes accessed | tf_op | source)
XLA Modules:
  0.0 103.8 jit_solution(820536602431625842)
XLA Ops:
  0.0 0.8 copy.8.corner
  0.8 2.8 %shard_map.73 = bf16[768,512]{1,0:T(8,128)(2,1)} custom-call(s32[384]{0:T(512)} %subgrid.1, s32[384]{0:T(512)} %plane.1, bf16[384,256]{1,0:T(8,128)(2,1)} %vis.1, bf16[384,128]{1,0:T(8,128)(2,1)} %weight.1, s32[2,384]{1,0:T(2,128)} %bitcast.8, s32[2,384]{1,0:T(2,128)} %bitcast.9), custom_call_target="tpu_custom_call" | custom-call | tf_op jit(solution)/shard_map/pallas_call | solution.py:248
  3.5 0.0 copy-start
  3.5 1.1 %copy-done = bf16[768,512]{1,0:T(8,128)(2,1)S(1)} copy-done((bf16[768,512]{1,0:T(8,128)(2,1)S(1)}, bf16[768,512]{1,0:T(8,128)(2,1)}, u32[]{:S(2)}) %copy-start) | copy-done | bytes 786456
  4.7 20.3 %shard_map.74 = bf16[32,24,512]{2,1,0:T(8,128)(2,1)S(1)} custom-call(bf16[32,24,512]{2,1,0:T(8,128)(2,1)S(1)} %bitcast.7), custom_call_target="tpu_custom_call" | custom-call | tf_op jit(solution)/shard_map/pallas_call | solution.py:265
  24.9 1.9 %shard_map.75 = (f32[768,256]{1,0:T(8,128)S(1)}, s32[768,256]{1,0:T(8,128)S(1)}, s32[3]{0:T(128)S(1)}) custom-call(bf16[768,512]{1,0:T(8,128)(2,1)S(1)} %bitcast.6), custom_call_target="tpu_custom_call" | custom-call | tf_op jit(solution)/shard_map/pallas_call | solution.py:277
  26.8 12.8 %shard_map.76 = (f32[2,128,256]{2,1,0:T(8,128)S(1)}, bf16[2,128,256]{2,1,0:T(8,128)(2,1)S(1)}, bf16[2,128,256]{2,1,0:T(8,128)(2,1)S(1)}) custom-call(f32[768,256]{1,0:T(8,128)S(1)} %get-tuple-element.17.scaled, s32[768,256]{1,0:T(8,128)S(1)} %get-tuple-element.18.position, s32[3]{0:T(128)S(1)} %get-tuple-element.19.counts, s32[3,2]{1,0:T(4,128)S(1)} %copy.8.corner), custom_call_target="tpu_custom_call" | custom-call | flops 1000 | bytes 1000 | tf_op jit(solution)/shard_map/pallas_call | solution.py:294
  39.6 4.3 %collective-permute-start.2 = (bf16[2,128,256]{2,1,0:T(8,128)(2,1)S(1)}, bf16[2,128,256]{2,1,0:T(8,128)(2,1)S(1)}, u32[]{:S(2)}, u32[]{:S(2)}) collective-permute-start(bf16[2,128,256]{2,1,0:T(8,128)(2,1)S(1)} %get-tuple-element.22), channel_id=1, source_target_pairs={{28,0},{0,4},{4,8},{8,12},{12,16},{16,20},{20,24},{24,28},{29,1},{... | collective-permute-start | bytes 393224 | tf_op jit(solution)/shard_map/ppermute | solution.py:315
  43.9 0.6 collective-permute-start.3
  44.5 0.7 slice_bitcast_fusion
  45.2 0.7 collective-permute-start.1
  45.9 3.4 %collective-permute-start = (s32[3]{0:T(128)S(1)}, s32[3]{0:T(128)S(1)}, u32[]{:S(2)}, u32[]{:S(2)}) collective-permute-start(s32[3]{0:T(128)S(1)} %slice_bitcast_fusion), channel_id=1, source_target_pairs={{28,0},{0,4},{4,8},{8,12},{12,16},{16,20},{20,24},{24,28},{29,1},{... | collective-permute-start | bytes 44 | tf_op jit(solution)/shard_map/ppermute | solution.py:245
  49.3 3.3 %collective-permute-done.1.refs_1_ = s32[3]{0:T(128)S(1)} collective-permute-done((s32[3]{0:T(128)S(1)}, s32[3]{0:T(128)S(1)}, u32[]{:S(2)}, u32[]{:S(2)}) %collective-permute-start.1) | collective-permute-done | bytes 44 | tf_op jit(solution)/shard_map/ppermute | solution.py:246
  52.7 0.0 collective-permute-done.refs_0_
  52.7 24.1 %shard_map.77 = (f32[2,128,256]{2,1,0:T(8,128)S(1)}, bf16[2,128,256]{2,1,0:T(8,128)(2,1)S(1)}, bf16[2,128,256]{2,1,0:T(8,128)(2,1)S(1)}) custom-call(f32[768,256]{1,0:T(8,128)S(1)} %get-tuple-element.17.scaled, s32[768,256]{1,0:T(8,128)S(1)} %get-tuple-element.18.position, s32[3]{0:T(128)S(1)} %get-tuple-element.19.counts, s32[3,2]{1,0:T(4,128)S(1)} %copy.8.corner, ...), custom_call_target="tpu_custom_call" | custom-call | flops 1000 | bytes 1000 | tf_op jit(solution)/shard_map/pallas_call | solution.py:294
  76.8 0.1 collective-permute-start.4
  76.8 0.1 collective-permute-start.6
  76.9 0.0 collective-permute-done.2.refs_0_.refs_3_
  76.9 0.0 collective-permute-done.3.refs_1_.refs_6_
  76.9 12.8 %shard_map.78 = (f32[2,128,256]{2,1,0:T(8,128)S(1)}, bf16[2,128,256]{2,1,0:T(8,128)(2,1)S(1)}, bf16[2,128,256]{2,1,0:T(8,128)(2,1)S(1)}) custom-call(f32[768,256]{1,0:T(8,128)S(1)} %get-tuple-element.17.scaled, s32[768,256]{1,0:T(8,128)S(1)} %get-tuple-element.18.position, s32[3]{0:T(128)S(1)} %get-tuple-element.19.counts, s32[3,2]{1,0:T(4,128)S(1)} %copy.8.corner, ...), custom_call_target="tpu_custom_call" | custom-call | flops 1000 | bytes 1000 | tf_op jit(solution)/shard_map/pallas_call | solution.py:294
  89.7 0.1 collective-permute-start.5
  89.8 0.1 collective-permute-start.7
  89.8 0.1 pad_add_fusion.columns
  89.9 0.0 collective-permute-done.4.refs_4_
  89.9 0.0 collective-permute-done.6.refs_7_
  89.9 4.8 %collective-permute-done.5.refs_5_ = bf16[2,128,256]{2,1,0:T(8,128)(2,1)S(1)} collective-permute-done((bf16[2,128,256]{2,1,0:T(8,128)(2,1)S(1)}, bf16[2,128,256]{2,1,0:T(8,128)(2,1)S(1)}, u32[]{:S(2)}, u32[]{:S(2)}) %collective-permute-start.5) | collective-permute-done | bytes 131104 | tf_op jit(solution)/shard_map/ppermute | solution.py:315
  94.7 4.6 %collective-permute-done.7.refs_8_ = bf16[2,128,256]{2,1,0:T(8,128)(2,1)S(1)} collective-permute-done((bf16[2,128,256]{2,1,0:T(8,128)(2,1)S(1)}, bf16[2,128,256]{2,1,0:T(8,128)(2,1)S(1)}, u32[]{:S(2)}, u32[]{:S(2)}) %collective-permute-start.7) | collective-permute-done | bytes 131104 | tf_op jit(solution)/shard_map/ppermute | solution.py:316
  99.3 4.5 %shard_map.79 = f32[1,2,128,8192]{3,2,1,0:T(8,128)} custom-call(s32[9]{0:T(128)S(1)} %pad_add_fusion.columns, f32[2,128,256]{2,1,0:T(8,128)S(1)} %get-tuple-element.20.refs_0_, f32[2,128,256]{2,1,0:T(8,128)S(1)} %get-tuple-element.21.refs_1_, f32[2,128,256]{2,1,0:T(8,128)S(1)} %get-tuple-element.24.refs_2_, ...), custom_call_target="tpu_custom_call" | custom-call | tf_op jit(solution)/shard_map/pallas_call | solution.py:321
Async XLA Ops:
  3.5 1.1 %copy-start = (bf16[768,512]{1,0:T(8,128)(2,1)S(1)}, bf16[768,512]{1,0:T(8,128)(2,1)}, u32[]{:S(2)}) copy-start(bf16[768,512]{1,0:T(8,128)(2,1)} %shard_map.73) | copy-start | bytes 2359300
  39.6 37.3 %collective-permute-start.2 = (bf16[2,128,256]{2,1,0:T(8,128)(2,1)S(1)}, bf16[2,128,256]{2,1,0:T(8,128)(2,1)S(1)}, u32[]{:S(2)}, u32[]{:S(2)}) collective-permute-start(bf16[2,128,256]{2,1,0:T(8,128)(2,1)S(1)} %get-tuple-element.22), channel_id=1, source_target_pairs={{28,0},{0,4},{4,8},{8,12},{12,16},{16,20},{20,24},{24,28},{29,1},{... | collective-permute-start | bytes 393224 | tf_op jit(solution)/shard_map/ppermute | solution.py:315
  43.9 33.0 %collective-permute-start.3 = (bf16[2,128,256]{2,1,0:T(8,128)(2,1)S(1)}, bf16[2,128,256]{2,1,0:T(8,128)(2,1)S(1)}, u32[]{:S(2)}, u32[]{:S(2)}) collective-permute-start(bf16[2,128,256]{2,1,0:T(8,128)(2,1)S(1)} %get-tuple-element.23), channel_id=1, source_target_pairs={{24,0},{28,4},{0,8},{4,12},{8,16},{12,20},{16,24},{20,28},{25,1},{... | collective-permute-start | bytes 393224 | tf_op jit(solution)/shard_map/ppermute | solution.py:316
  45.2 7.5 %collective-permute-start.1 = (s32[3]{0:T(128)S(1)}, s32[3]{0:T(128)S(1)}, u32[]{:S(2)}, u32[]{:S(2)}) collective-permute-start(s32[3]{0:T(128)S(1)} %slice_bitcast_fusion), channel_id=1, source_target_pairs={{24,0},{28,4},{0,8},{4,12},{8,16},{12,20},{16,24},{20,28},{25,1},{... | collective-permute-start | bytes 44 | tf_op jit(solution)/shard_map/ppermute | solution.py:246
  45.9 6.8 %collective-permute-start = (s32[3]{0:T(128)S(1)}, s32[3]{0:T(128)S(1)}, u32[]{:S(2)}, u32[]{:S(2)}) collective-permute-start(s32[3]{0:T(128)S(1)} %slice_bitcast_fusion), channel_id=1, source_target_pairs={{28,0},{0,4},{4,8},{8,12},{12,16},{16,20},{20,24},{24,28},{29,1},{... | collective-permute-start | bytes 44 | tf_op jit(solution)/shard_map/ppermute | solution.py:245
  76.8 13.1 %collective-permute-start.4 = (bf16[2,128,256]{2,1,0:T(8,128)(2,1)S(1)}, bf16[2,128,256]{2,1,0:T(8,128)(2,1)S(1)}, u32[]{:S(2)}, u32[]{:S(2)}) collective-permute-start(bf16[2,128,256]{2,1,0:T(8,128)(2,1)S(1)} %get-tuple-element.25), channel_id=1, source_target_pairs={{28,0},{0,4},{4,8},{8,12},{12,16},{16,20},{20,24},{24,28},{29,1},{... | collective-permute-start | bytes 393224 | tf_op jit(solution)/shard_map/ppermute | solution.py:315
  76.8 13.1 %collective-permute-start.6 = (bf16[2,128,256]{2,1,0:T(8,128)(2,1)S(1)}, bf16[2,128,256]{2,1,0:T(8,128)(2,1)S(1)}, u32[]{:S(2)}, u32[]{:S(2)}) collective-permute-start(bf16[2,128,256]{2,1,0:T(8,128)(2,1)S(1)} %get-tuple-element.27), channel_id=1, source_target_pairs={{24,0},{28,4},{0,8},{4,12},{8,16},{12,20},{16,24},{20,28},{25,1},{... | collective-permute-start | bytes 393224 | tf_op jit(solution)/shard_map/ppermute | solution.py:316
  89.7 5.0 %collective-permute-start.5 = (bf16[2,128,256]{2,1,0:T(8,128)(2,1)S(1)}, bf16[2,128,256]{2,1,0:T(8,128)(2,1)S(1)}, u32[]{:S(2)}, u32[]{:S(2)}) collective-permute-start(bf16[2,128,256]{2,1,0:T(8,128)(2,1)S(1)} %get-tuple-element.26), channel_id=1, source_target_pairs={{28,0},{0,4},{4,8},{8,12},{12,16},{16,20},{20,24},{24,28},{29,1},{... | collective-permute-start | bytes 393224 | tf_op jit(solution)/shard_map/ppermute | solution.py:315
  89.8 9.5 %collective-permute-start.7 = (bf16[2,128,256]{2,1,0:T(8,128)(2,1)S(1)}, bf16[2,128,256]{2,1,0:T(8,128)(2,1)S(1)}, u32[]{:S(2)}, u32[]{:S(2)}) collective-permute-start(bf16[2,128,256]{2,1,0:T(8,128)(2,1)S(1)} %get-tuple-element.28), channel_id=1, source_target_pairs={{24,0},{28,4},{0,8},{4,12},{8,16},{12,20},{16,24},{20,28},{25,1},{... | collective-permute-start | bytes 393224 | tf_op jit(solution)/shard_map/ppermute | solution.py:316
where the time goes:
time: 102 us; the launch traced here: 104 us
  Pallas kernels  79 us (77%)
  waiting for transfers between devices  12.7 us (12%)
  starting transfers between devices  9.27 us (9%)
  local copies, waits for them, and re-layouts  2.58 us (3%)
    pallas_call x3, Pallas kernels, shards(): pl.pallas_call(functools.partial(grid_kernel, m), grid=(1,), out_shape=(j...  49.6 us
    pallas_call x1, Pallas kernels, shards(): pl.pallas_call(functools.partial(exchange_kernel, sub_count, fac_count),...  20.3 us
    ppermute x3, waiting for transfers between devices, shards(): nears.append(lax.ppermute(near, 'sub', ring(1)))  4.81 us
    ppermute x3, waiting for transfers between devices, shards(): fars.append(lax.ppermute(far, 'sub', ring(2)))  4.58 us
    pallas_call x1, Pallas kernels, shards(): pl.pallas_call(functools.partial(place_kernel, 3 * members), grid=(2, BAN...  4.49 us
    ppermute x3, starting transfers between devices, shards(): nears.append(lax.ppermute(near, 'sub', ring(1)))  4.41 us
    ppermute x1, starting transfers between devices, shards(): next_cols = lax.ppermute(columns, 'sub', ring(1))  3.44 us
    ppermute x1, waiting for transfers between devices, shards(): far_cols = lax.ppermute(columns, 'sub', ring(2))  3.34 us
  transfers between devices with their start and end apart: 8, of which 3 were waited for; matrix products, arithmetic and copies ran while one was open for 1% of the time, Pallas kernels for 35%

commit v1 on v0

--- a/solution.py
+++ b/solution.py
@@ -35,7 +35,7 @@
     return lax.dot_general(a, b, dims, preferred_element_type=jnp.float32)
 
 
-def pack_kernel(capacity, dest_count, members, planes, subgrid, plane, vis, weight, start, step, packet):
+def pack_kernel(capacity, dest_count, members, planes, corner, subgrid, plane, vis, weight, start, step, packet):
     rows = vis.shape[0]
     slots = packet.shape[0]
     subgrids, w_planes = subgrid[...].reshape(1, rows), plane[...].reshape(1, rows)
@@ -61,7 +61,13 @@
     track = value.astype(jnp.float32).astype(jnp.bfloat16)
     packet[:, 0 : 2 * LANES] = dot(place, vis[...]).astype(jnp.bfloat16)
     packet[:, 2 * LANES : 3 * LANES] = dot(place, weight[...]).astype(jnp.bfloat16)
-    packet[:, 3 * LANES : 4 * LANES] = dot(place, track, NT).astype(jnp.bfloat16)
+    spare = iota((1, LANES), 1)
+    columns = jnp.zeros((1, LANES), jnp.int32)
+    for m in range(members):
+        columns = jnp.where(spare == 11 + 2 * m, corner[m, 1] & 255, columns)
+        columns = jnp.where(spare == 12 + 2 * m, lax.shift_right_logical(corner[m, 1], 8), columns)
+    packed = dot(place, track, NT) + columns.astype(jnp.float32)
+    packet[:, 3 * LANES : 4 * LANES] = packed.astype(jnp.bfloat16)
 
 
 def exchange_kernel(sub_count, fac_count, source, landed, send_sem, recv_sem, own_sem):
@@ -108,7 +114,7 @@
     own.wait()
 
 
-def sort_kernel(capacity, members, packet, scaled, position, counts):
+def sort_kernel(capacity, members, sub_count, fac_count, packet, scaled, position, counts, places):
     slots = packet.shape[0]
     part = slots // members
     track = packet[:, 3 * LANES : 4 * LANES]
@@ -125,6 +131,14 @@
     place = onehot(iota((slots, slots), 0) == goal)
     for m in range(members):
         counts[m] = jnp.sum(jnp.where((member == m) & (used > 0.5), 1, 0))
+    lane = iota((8, LANES), 1)
+    for behind in range(3):
+        origin = lax.rem(lax.axis_index("sub") + 2 * sub_count - behind, sub_count) * fac_count
+        line = onehot(iota((8, slots), 1) == origin * members * capacity)
+        line = jnp.where(iota((8, LANES), 0) == 0, dot(line, track), 0.0).astype(jnp.int32)
+        for m in range(members):
+            column = jnp.where(lane == 11 + 2 * m, line, jnp.where(lane == 12 + 2 * m, line * 256, 0))
+            places[behind * members + m] = jnp.sum(column)
     weight = dot(place, packet[:, 2 * LANES : 3 * LANES])
     scaled[:, 0:LANES] = dot(place, packet[:, 0:LANES]) * weight
     scaled[:, LANES : 2 * LANES] = dot(place, packet[:, LANES : 2 * LANES]) * weight
@@ -240,16 +254,13 @@
     part = slots // members
     smem = pl.BlockSpec(memory_space=pltpu.SMEM)
 
-    columns = tile_intersection[:, 1]
     ring = lambda d: [((i - d) % sub_count, i) for i in range(sub_count)]
-    next_cols = lax.ppermute(columns, "sub", ring(1))
-    far_cols = lax.ppermute(columns, "sub", ring(2))
-
     packet = pl.pallas_call(
         functools.partial(pack_kernel, capacity, dest_count, members, fac_count),
         out_shape=jax.ShapeDtypeStruct((slots, 4 * LANES), jnp.bfloat16),
         grid=(1,),
         in_specs=[
+            smem,
             pl.BlockSpec((rows,), lambda i: (0,)),
             pl.BlockSpec((rows,), lambda i: (0,)),
             pl.BlockSpec((rows, 2 * chans), lambda i: (0, 0)),
@@ -259,7 +270,7 @@
         ],
         out_specs=pl.BlockSpec((slots, 4 * LANES), lambda i: (0, 0)),
         compiler_params=params(PACK_LIMIT),
-    )(subgrid_id, w_plane, visibility, vis_weight, tap_start.T, tap_step.T)
+    )(tile_intersection, subgrid_id, w_plane, visibility, vis_weight, tap_start.T, tap_step.T)
     devices = sub_count * fac_count
     blocks = jax.ShapeDtypeStruct((devices, members * capacity, 4 * LANES), jnp.bfloat16)
     packet = pl.pallas_call(
@@ -274,21 +285,22 @@
         ],
         compiler_params=params(collective_id=0, has_side_effects=True),
     )(packet.reshape(blocks.shape)).reshape(slots, 4 * LANES)
-    scaled, position, counts = pl.pallas_call(
-        functools.partial(sort_kernel, capacity, members),
+    scaled, position, counts, places = pl.pallas_call(
+        functools.partial(sort_kernel, capacity, members, sub_count, fac_count),
         out_shape=(
             jax.ShapeDtypeStruct((slots, 2 * LANES), jnp.float32),
             jax.ShapeDtypeStruct((slots, 2 * LANES), jnp.int32),
             jax.ShapeDtypeStruct((members,), jnp.int32),
+            jax.ShapeDtypeStruct((3 * members,), jnp.int32),
         ),
         in_specs=whole(1),
-        out_specs=(*whole(2), smem),
+        out_specs=(*whole(2), smem, smem),
         compiler_params=params(),
     )(packet)
 
     owns, nears, fars = [], [], []
     for m in range(members):
-        arrived = (nears[m - 2], fars[m - 2]) if m >= 2 else (next_cols, far_cols) if m == 1 else ()
+        arrived = (nears[m - 2], fars[m - 2]) if m >= 2 else ()
         block = pl.BlockSpec((part, 2 * LANES), lambda i, m=m: (m, 0))
         piece = pl.BlockSpec((2, BAND, SG), lambda i: (0, 0, 0))
         own, near, far = pl.pallas_call(
@@ -315,7 +327,6 @@
         nears.append(lax.ppermute(near, "sub", ring(1)))
         fars.append(lax.ppermute(far, "sub", ring(2)))
 
-    places = jnp.concatenate([columns, next_cols, far_cols])
     high = 64
     cut = pl.BlockSpec((1, high, SG), lambda p, i: (p, i, 0))
     return pl.pallas_call(

time: 102 us -> 99.5 us (0.975)
  the two profiles are of different devices: /device:TPU:6 before, /device:TPU:0 now
where the time goes in v1:
time: 99.5 us; the launch traced here: 100 us
  Pallas kernels  68.2 us (69%)
  starting transfers between devices  22.1 us (22%)
  waiting for transfers between devices  6.76 us (7%)
  local copies, waits for them, and re-layouts  3.12 us (3%)
    pallas_call x3, Pallas kernels, shards(): pl.pallas_call(functools.partial(grid_kernel, m), grid=(1,), out_shape=(j...  38.3 us
    pallas_call x1, Pallas kernels, shards(): pl.pallas_call(functools.partial(exchange_kernel, sub_count, fac_count),...  20.7 us
    ppermute x3, starting transfers between devices, shards(): nears.append(lax.ppermute(near, 'sub', ring(1)))  17.4 us
    ppermute x3, starting transfers between devices, shards(): fars.append(lax.ppermute(far, 'sub', ring(2)))  4.73 us
    pallas_call x1, Pallas kernels, shards(): pl.pallas_call(functools.partial(place_kernel, 3 * members), grid=(2, BAN...  4.49 us
    ppermute x3, waiting for transfers between devices, shards(): fars.append(lax.ppermute(far, 'sub', ring(2)))  4.25 us
    unnamed x5, local copies, waits for them, and re-layouts  3.12 us
    pallas_call x1, Pallas kernels, shards(): pl.pallas_call(functools.partial(pack_kernel, capacity, dest_count, membe...  2.76 us
  transfers between devices with their start and end apart: 6, of which 2 were waited for; matrix products, arithmetic and copies ran while one was open for 0% of the time, Pallas kernels for 27%

profile of v1, /device:TPU:0, one launch (start us, length us, event | category | flops | bytes accessed | tf_op | source)
XLA Modules:
  0.0 100.2 jit_solution(3915639908640407065)
XLA Ops:
  0.0 1.3 %copy.8.corner = s32[3,2]{1,0:T(4,128)} copy(s32[3,2]{0,1:T(2,128)} %param.13) | data formatting | bytes 48 | tf_op args[6]
  1.3 2.8 %shard_map.73 = bf16[768,512]{1,0:T(8,128)(2,1)} custom-call(s32[3,2]{1,0:T(4,128)} %copy.8.corner, s32[384]{0:T(512)} %subgrid.1, s32[384]{0:T(512)} %plane.1, bf16[384,256]{1,0:T(8,128)(2,1)} %vis.1, bf16[384,128]{1,0:T(8,128)(2,1)} %weight.1, s32[2,384]{1,0:T(2,128)} %bitcast.6, s32[2,384]{1,0:T(2,128)} %bitcast.7), custom_call_target="tpu_custom_call" | custom-call | tf_op jit(solution)/shard_map/pallas_call | solution.py:258
  4.1 0.0 copy-start
  4.1 1.1 %copy-done = bf16[768,512]{1,0:T(8,128)(2,1)S(1)} copy-done((bf16[768,512]{1,0:T(8,128)(2,1)S(1)}, bf16[768,512]{1,0:T(8,128)(2,1)}, u32[]{:S(2)}) %copy-start) | copy-done | bytes 786456
  5.2 20.7 %shard_map.74 = bf16[32,24,512]{2,1,0:T(8,128)(2,1)S(1)} custom-call(bf16[32,24,512]{2,1,0:T(8,128)(2,1)S(1)} %bitcast.5), custom_call_target="tpu_custom_call" | custom-call | tf_op jit(solution)/shard_map/pallas_call | solution.py:276
  26.0 1.9 %shard_map.75 = (f32[768,256]{1,0:T(8,128)S(1)}, s32[768,256]{1,0:T(8,128)S(1)}, s32[3]{0:T(128)S(1)}, s32[9]{0:T(128)S(1)}) custom-call(bf16[768,512]{1,0:T(8,128)(2,1)S(1)} %bitcast.4), custom_call_target="tpu_custom_call" | custom-call | tf_op jit(solution)/shard_map/pallas_call | solution.py:288
  27.9 0.0 copy-start.1
  27.9 0.7 copy-done.1
  28.5 11.4 %shard_map.76 = (f32[2,128,256]{2,1,0:T(8,128)S(1)}, bf16[2,128,256]{2,1,0:T(8,128)(2,1)S(1)}, bf16[2,128,256]{2,1,0:T(8,128)(2,1)S(1)}) custom-call(f32[768,256]{1,0:T(8,128)S(1)} %get-tuple-element.19.scaled, s32[768,256]{1,0:T(8,128)S(1)} %get-tuple-element.20.position, s32[3]{0:T(128)S(1)} %get-tuple-element.21.counts, s32[3,2]{1,0:T(4,128)S(1)} %copy-done.1), custom_call_target="tpu_custom_call" | custom-call | flops 1000 | bytes 1000 | tf_op jit(solution)/shard_map/pallas_call | solution.py:306
  39.9 3.4 %collective-permute-start = (bf16[2,128,256]{2,1,0:T(8,128)(2,1)S(1)}, bf16[2,128,256]{2,1,0:T(8,128)(2,1)S(1)}, u32[]{:S(2)}, u32[]{:S(2)}) collective-permute-start(bf16[2,128,256]{2,1,0:T(8,128)(2,1)S(1)} %get-tuple-element.24), channel_id=1, source_target_pairs={{28,0},{0,4},{4,8},{8,12},{12,16},{16,20},{20,24},{24,28},{29,1},{... | collective-permute-start | bytes 393224 | tf_op jit(solution)/shard_map/ppermute | solution.py:327
  43.2 4.7 %collective-permute-start.1 = (bf16[2,128,256]{2,1,0:T(8,128)(2,1)S(1)}, bf16[2,128,256]{2,1,0:T(8,128)(2,1)S(1)}, u32[]{:S(2)}, u32[]{:S(2)}) collective-permute-start(bf16[2,128,256]{2,1,0:T(8,128)(2,1)S(1)} %get-tuple-element.25), channel_id=1, source_target_pairs={{24,0},{28,4},{0,8},{4,12},{8,16},{12,20},{16,24},{20,28},{25,1},{... | collective-permute-start | bytes 393224 | tf_op jit(solution)/shard_map/ppermute | solution.py:328
  48.0 12.8 %shard_map.77 = (f32[2,128,256]{2,1,0:T(8,128)S(1)}, bf16[2,128,256]{2,1,0:T(8,128)(2,1)S(1)}, bf16[2,128,256]{2,1,0:T(8,128)(2,1)S(1)}) custom-call(f32[768,256]{1,0:T(8,128)S(1)} %get-tuple-element.19.scaled, s32[768,256]{1,0:T(8,128)S(1)} %get-tuple-element.20.position, s32[3]{0:T(128)S(1)} %get-tuple-element.21.counts, s32[3,2]{1,0:T(4,128)S(1)} %copy-done.1), custom_call_target="tpu_custom_call" | custom-call | flops 1000 | bytes 1000 | tf_op jit(solution)/shard_map/pallas_call | solution.py:306
  60.7 1.7 %collective-permute-start.2 = (bf16[2,128,256]{2,1,0:T(8,128)(2,1)S(1)}, bf16[2,128,256]{2,1,0:T(8,128)(2,1)S(1)}, u32[]{:S(2)}, u32[]{:S(2)}) collective-permute-start(bf16[2,128,256]{2,1,0:T(8,128)(2,1)S(1)} %get-tuple-element.27), channel_id=1, source_target_pairs={{28,0},{0,4},{4,8},{8,12},{12,16},{16,20},{20,24},{24,28},{29,1},{... | collective-permute-start | bytes 393224 | tf_op jit(solution)/shard_map/ppermute | solution.py:327
  62.4 0.0 collective-permute-start.4
  62.5 0.0 collective-permute-done.refs_0_.refs_3_
  62.5 0.0 collective-permute-done.1.refs_1_.refs_6_
  62.5 14.2 %shard_map.78 = (f32[2,128,256]{2,1,0:T(8,128)S(1)}, bf16[2,128,256]{2,1,0:T(8,128)(2,1)S(1)}, bf16[2,128,256]{2,1,0:T(8,128)(2,1)S(1)}) custom-call(f32[768,256]{1,0:T(8,128)S(1)} %get-tuple-element.19.scaled, s32[768,256]{1,0:T(8,128)S(1)} %get-tuple-element.20.position, s32[3]{0:T(128)S(1)} %get-tuple-element.21.counts, s32[3,2]{1,0:T(4,128)S(1)} %copy-done.1, ...), custom_call_target="tpu_custom_call" | custom-call | flops 1000 | bytes 1000 | tf_op jit(solution)/shard_map/pallas_call | solution.py:306
  76.7 12.3 %collective-permute-start.3 = (bf16[2,128,256]{2,1,0:T(8,128)(2,1)S(1)}, bf16[2,128,256]{2,1,0:T(8,128)(2,1)S(1)}, u32[]{:S(2)}, u32[]{:S(2)}) collective-permute-start(bf16[2,128,256]{2,1,0:T(8,128)(2,1)S(1)} %get-tuple-element.28), channel_id=1, source_target_pairs={{28,0},{0,4},{4,8},{8,12},{12,16},{16,20},{20,24},{24,28},{29,1},{... | collective-permute-start | bytes 393224 | tf_op jit(solution)/shard_map/ppermute | solution.py:327
  89.0 0.0 collective-permute-start.5
  89.0 0.0 collective-permute-done.2.refs_4_
  89.0 0.0 collective-permute-done.4.refs_7_
  89.0 2.5 %collective-permute-done.3.refs_5_ = bf16[2,128,256]{2,1,0:T(8,128)(2,1)S(1)} collective-permute-done((bf16[2,128,256]{2,1,0:T(8,128)(2,1)S(1)}, bf16[2,128,256]{2,1,0:T(8,128)(2,1)S(1)}, u32[]{:S(2)}, u32[]{:S(2)}) %collective-permute-start.3) | collective-permute-done | bytes 131104 | tf_op jit(solution)/shard_map/ppermute | solution.py:327
  91.5 4.2 %collective-permute-done.5.refs_8_ = bf16[2,128,256]{2,1,0:T(8,128)(2,1)S(1)} collective-permute-done((bf16[2,128,256]{2,1,0:T(8,128)(2,1)S(1)}, bf16[2,128,256]{2,1,0:T(8,128)(2,1)S(1)}, u32[]{:S(2)}, u32[]{:S(2)}) %collective-permute-start.5) | collective-permute-done | bytes 131104 | tf_op jit(solution)/shard_map/ppermute | solution.py:328
  95.7 4.5 %shard_map.79 = f32[1,2,128,8192]{3,2,1,0:T(8,128)} custom-call(s32[9]{0:T(128)S(1)} %get-tuple-element.18.columns, f32[2,128,256]{2,1,0:T(8,128)S(1)} %get-tuple-element.22.refs_0_, f32[2,128,256]{2,1,0:T(8,128)S(1)} %get-tuple-element.23.refs_1_, f32[2,128,256]{2,1,0:T(8,128)S(1)} %get-tuple-element.26.refs_2_, ...), custom_call_target="tpu_custom_call" | custom-call | tf_op jit(solution)/shard_map/pallas_call | solution.py:332
Async XLA Ops:
  4.1 1.1 %copy-start = (bf16[768,512]{1,0:T(8,128)(2,1)S(1)}, bf16[768,512]{1,0:T(8,128)(2,1)}, u32[]{:S(2)}) copy-start(bf16[768,512]{1,0:T(8,128)(2,1)} %shard_map.73) | copy-start | bytes 2359300
  27.9 0.7 copy-start.1
  39.9 22.6 %collective-permute-start = (bf16[2,128,256]{2,1,0:T(8,128)(2,1)S(1)}, bf16[2,128,256]{2,1,0:T(8,128)(2,1)S(1)}, u32[]{:S(2)}, u32[]{:S(2)}) collective-permute-start(bf16[2,128,256]{2,1,0:T(8,128)(2,1)S(1)} %get-tuple-element.24), channel_id=1, source_target_pairs={{28,0},{0,4},{4,8},{8,12},{12,16},{16,20},{20,24},{24,28},{29,1},{... | collective-permute-start | bytes 393224 | tf_op jit(solution)/shard_map/ppermute | solution.py:327
  43.2 19.2 %collective-permute-start.1 = (bf16[2,128,256]{2,1,0:T(8,128)(2,1)S(1)}, bf16[2,128,256]{2,1,0:T(8,128)(2,1)S(1)}, u32[]{:S(2)}, u32[]{:S(2)}) collective-permute-start(bf16[2,128,256]{2,1,0:T(8,128)(2,1)S(1)} %get-tuple-element.25), channel_id=1, source_target_pairs={{24,0},{28,4},{0,8},{4,12},{8,16},{12,20},{16,24},{20,28},{25,1},{... | collective-permute-start | bytes 393224 | tf_op jit(solution)/shard_map/ppermute | solution.py:328
  60.7 28.3 %collective-permute-start.2 = (bf16[2,128,256]{2,1,0:T(8,128)(2,1)S(1)}, bf16[2,128,256]{2,1,0:T(8,128)(2,1)S(1)}, u32[]{:S(2)}, u32[]{:S(2)}) collective-permute-start(bf16[2,128,256]{2,1,0:T(8,128)(2,1)S(1)} %get-tuple-element.27), channel_id=1, source_target_pairs={{28,0},{0,4},{4,8},{8,12},{12,16},{16,20},{20,24},{24,28},{29,1},{... | collective-permute-start | bytes 393224 | tf_op jit(solution)/shard_map/ppermute | solution.py:327
  62.4 26.5 %collective-permute-start.4 = (bf16[2,128,256]{2,1,0:T(8,128)(2,1)S(1)}, bf16[2,128,256]{2,1,0:T(8,128)(2,1)S(1)}, u32[]{:S(2)}, u32[]{:S(2)}) collective-permute-start(bf16[2,128,256]{2,1,0:T(8,128)(2,1)S(1)} %get-tuple-element.29), channel_id=1, source_target_pairs={{24,0},{28,4},{0,8},{4,12},{8,16},{12,20},{16,24},{20,28},{25,1},{... | collective-permute-start | bytes 393224 | tf_op jit(solution)/shard_map/ppermute | solution.py:328
  76.7 14.9 %collective-permute-start.3 = (bf16[2,128,256]{2,1,0:T(8,128)(2,1)S(1)}, bf16[2,128,256]{2,1,0:T(8,128)(2,1)S(1)}, u32[]{:S(2)}, u32[]{:S(2)}) collective-permute-start(bf16[2,128,256]{2,1,0:T(8,128)(2,1)S(1)} %get-tuple-element.28), channel_id=1, source_target_pairs={{28,0},{0,4},{4,8},{8,12},{12,16},{16,20},{20,24},{24,28},{29,1},{... | collective-permute-start | bytes 393224 | tf_op jit(solution)/shard_map/ppermute | solution.py:327
  89.0 6.8 %collective-permute-start.5 = (bf16[2,128,256]{2,1,0:T(8,128)(2,1)S(1)}, bf16[2,128,256]{2,1,0:T(8,128)(2,1)S(1)}, u32[]{:S(2)}, u32[]{:S(2)}) collective-permute-start(bf16[2,128,256]{2,1,0:T(8,128)(2,1)S(1)} %get-tuple-element.30), channel_id=1, source_target_pairs={{24,0},{28,4},{0,8},{4,12},{8,16},{12,20},{16,24},{20,28},{25,1},{... | collective-permute-start | bytes 393224 | tf_op jit(solution)/shard_map/ppermute | solution.py:328
